TPU v7x, 32 devices: a whole 2x2x4 slice. The times are simulated.
32 devices in a mesh: row: 4 (over z), col: 8 (over y, x, core).
Axes of the slice: x: 2, y: 2, z: 4, core: 2. Of those that a mesh axis runs over, the one named last changes fastest.
Arguments:
- updates: float32 [16384, 8192], P('col', 'row'), may hold values from -6 to 6
- block_map: int32 [2, 64], replicated, may hold values from 0 to 79, as said below
- own_diag: float32 [10240], P('row'), may hold values from 2 to 6
- panel_inverse: float32 [512, 512], replicated, as said below
Outputs:
- factor_panel: float32 [10240, 512], P('row')
- trailing: float32 [10240, 10240], P('row', 'col')
Inputs may be any that keep to these rules, and one draw needn't show every extreme that they name: `block_map`: within one child the 64 entries name distinct front blocks. Take the child blocks (a, b) held by one device in updates, and the front blocks held by one device in trailing: either exactly 8 of the former land in the latter, or none do. `panel_inverse`: lower triangular with a positive diagonal.
All inputs are finite; a program needn't handle non-finite values.
Results may differ from a plain program's by a relative error of at most 0.000075.
Values sent between devices are 32-bit elements; how exact they have to be, the bound alone decides.
A program may use at most 128 MiB of HBM per device.

v0:
```python
import jax
import jax.numpy as jnp
from jax import lax
from jax.sharding import PartitionSpec as P

F = 10240
M = 8192
BLK = 128
PANEL = 512


def broadcast(shard, axis, root):
    mine = lax.axis_index(axis) == root
    return lax.psum(jnp.where(mine, shard, jnp.zeros_like(shard)), axis)


def item_routes(source_row, source_col, block_map, row_count, col_count):
    half_cols = col_count // 2
    row_items = 2 * M // col_count // BLK
    col_items = M // row_count // BLK
    front_rows = F // BLK // row_count
    front_cols = F // BLK // col_count
    child_map = jnp.take(block_map, source_col // half_cols, axis=0)
    row_parent = jnp.take(
        child_map, source_col % half_cols * row_items + jnp.arange(row_items, dtype=jnp.int32)
    )
    col_parent = jnp.take(
        child_map, source_row * col_items + jnp.arange(col_items, dtype=jnp.int32)
    )
    target_dev = (
        (row_parent // front_rows)[:, None] * col_count + (col_parent // front_cols)[None, :]
    ).reshape(-1)
    target_blk = (
        (row_parent % front_rows)[:, None] * front_cols + (col_parent % front_cols)[None, :]
    ).reshape(-1)
    position = jnp.arange(target_dev.shape[0], dtype=jnp.int32)
    same_target = (target_dev[:, None] == target_dev[None, :]) & (
        position[:, None] > position[None, :]
    )
    ranking = jnp.sum(same_target.astype(jnp.int32), axis=1)
    return (target_dev, ranking, target_blk)


def on_device(updates, block_map, own_diag, panel_inverse):
    row_count = lax.axis_size("row")
    col_count = lax.axis_size("col")
    row_index = lax.axis_index("row")
    col_index = lax.axis_index("col")
    devices_all = row_count * col_count
    local_rows, local_cols = updates.shape
    row_items = local_rows // BLK
    col_items = local_cols // BLK
    capacity = max(1, row_items // row_count) * max(1, col_items // col_count)
    front_rows = F // BLK // row_count
    front_cols = F // BLK // col_count
    slot_total = devices_all * capacity
    target_dev, ranking, unused_blk = item_routes(
        row_index, col_index, block_map, row_count, col_count
    )
    child_tiles = (
        updates.reshape(row_items, BLK, col_items, BLK)
        .transpose(0, 2, 1, 3)
        .reshape(row_items * col_items, BLK, BLK)
    )
    outgoing = (
        jnp.zeros((slot_total, BLK, BLK), jnp.float32)
        .at[target_dev * capacity + ranking]
        .set(child_tiles)
    )
    incoming = lax.all_to_all(
        outgoing.reshape(devices_all, capacity, BLK, BLK),
        ("row", "col"),
        split_axis=0,
        concat_axis=0,
        tiled=True,
    )
    sources = jnp.arange(devices_all, dtype=jnp.int32)
    all_dev, all_rank, all_blk = jax.vmap(
        lambda source_row, source_col: item_routes(
            source_row, source_col, block_map, row_count, col_count
        )
    )(sources // col_count, sources % col_count)
    myself = row_index * col_count + col_index
    slot_of = jnp.where(all_dev == myself, sources[:, None] * capacity + all_rank, slot_total)
    dump_slot = front_rows * front_cols
    slot_target = (
        jnp.full((slot_total + 1,), dump_slot, jnp.int32)
        .at[slot_of.reshape(-1)]
        .set(all_blk.reshape(-1))
    )
    slot_target = slot_target[:slot_total]
    assembled = (
        jnp.zeros((dump_slot + 1, BLK, BLK), jnp.float32)
        .at[slot_target]
        .add(incoming.reshape(slot_total, BLK, BLK))
    )
    height = front_rows * BLK
    col_width = front_cols * BLK
    front_local = (
        assembled[:dump_slot]
        .reshape(front_rows, front_cols, BLK, BLK)
        .transpose(0, 2, 1, 3)
        .reshape(height, col_width)
    )
    row_global = row_index * height + jnp.arange(height, dtype=jnp.int32)
    col_global = col_index * col_width + jnp.arange(col_width, dtype=jnp.int32)
    front_local = front_local + jnp.where(
        row_global[:, None] == col_global[None, :], own_diag[:, None], 0.0
    )
    raw_panel = broadcast(front_local[:, :PANEL], "col", 0)
    factor_panel = jnp.dot(
        raw_panel,
        panel_inverse.T,
        precision=lax.Precision.HIGHEST,
        preferred_element_type=jnp.float32,
    )
    gathered = lax.all_gather(factor_panel, "row", axis=0, tiled=True)
    across = lax.dynamic_slice_in_dim(gathered, col_index * col_width, col_width, 0)
    update_term = lax.dot_general(
        factor_panel,
        across,
        (((1,), (1,)), ((), ())),
        precision=lax.Precision.HIGHEST,
        preferred_element_type=jnp.float32,
    )
    trailing = front_local - update_term
    return (factor_panel, trailing)


def solution(mesh):
    return jax.shard_map(
        on_device,
        mesh=mesh,
        in_specs=(P("col", "row"), P(), P("row"), P()),
        out_specs=(P("row", None), P("row", "col")),
        check_vma=False,
    )
```

profile of v0, /device:TPU:8, one launch (start us, length us, event | category | flops | bytes accessed | tf_op | source)
XLA Modules:
  0.0 1047.4 jit_solution(4723716136499063705)
XLA Ops:
  7.2 0.8 fusion.15
  8.0 0.7 gather_fusion.3
  8.7 0.7 gather_fusion.4
  9.6 0.2 convert_reduce_fusion.1
  9.8 9.4 copy.44
  19.2 1.6 bitcast_bitcast_fusion
  20.8 7.8 copy.38
  28.6 7.8 broadcast_in_dim.89
  36.5 45.7 %scatter_fusion = f32[256,128,128]{2,1,0:T(8,128)} fusion(f32[256,128,128]{2,1,0:T(8,128)} %broadcast_in_dim.89, s32[256]{0:T(256)S(1)} %bitcast.50, f32[256,128,128]{2,1,0:T(8,128)} %bitcast.43), kind=kCustom, calls=%fused_computation.6 | custom fusion | bytes 50332672 | tf_op jit(solution)/shard_map/scatter | solution.py:68
  82.2 6.2 all-to-all-start
  88.6 0.1 reshape.447
  88.7 0.6 gather_fusion
  89.4 3.8 gather_fusion.1
  93.5 3.8 gather_fusion.2
  97.5 0.2 copy.33
  97.7 0.2 eq.71
  98.0 2.6 convert_reduce_fusion
  100.9 0.1 broadcast_add_fusion
  101.0 0.1 reshape.413
  101.2 30.6 %scatter_custom_fusion = s32[257]{0:T(512)S(1)} fusion(s32[8192]{0:T(1024)S(1)} %bitcast.49, s32[8192]{0:T(1024)S(1)} %reshape.413, s32[]{:T(128)} %constant.175.clone.1), kind=kCustom, calls=%fused_computation.77 | custom fusion | bytes 1032 | tf_op jit(solution)/shard_map/scatter | solution.py:89
  131.9 317.9 %all-to-all-done = f32[32,8,128,128]{3,2,1,0:T(8,128)} async-done(((f32[32,8,128,128]{3,2,1,0:T(8,128)}), f32[32,8,128,128]{3,2,1,0:T(8,128)}, u32[]{:S(2)}, u32[]{:S(2)}) %all-to-all-start) | async-done | bytes 16777248 | tf_op jit(solution)/shard_map/all_to_all | solution.py:70
  449.7 6.4 broadcast_in_dim.83
  456.1 52.7 %scatter_fusion.1 = f32[201,128,128]{2,1,0:T(8,128)} fusion(f32[201,128,128]{2,1,0:T(8,128)} %broadcast_in_dim.83, s32[256]{0:T(256)S(1)} %compare_select_fusion.4, f32[256,128,128]{2,1,0:T(8,128)} %bitcast.11), kind=kCustom, calls=%fused_computation.7 | custom fusion | flops 4194304 | bytes 50332672 | tf_op jit(solution)/shard_map/scatter-add | solution.py:95
  508.7 12.0 %slice.29 = f32[200,128,128]{2,1,0:T(8,128)} slice(f32[201,128,128]{2,1,0:T(8,128)} %scatter_fusion.1), slice={[0:200], [0:128], [0:128]} | slice | bytes 26214400 | tf_op jit(solution)/shard_map/slice | solution.py:100
  520.7 14.2 %copy.41 = f32[20,128,10,128]{3,2,1,0:T(8,128)S(1)} copy(f32[20,128,10,128]{3,1,2,0:T(8,128)} %bitcast.45) | data formatting | bytes 26214400 | tf_op jit(solution)/shard_map/reshape | solution.py:103
  534.9 7.4 bitcast_add_fusion
  542.3 5.5 slice_select_fusion
  547.8 0.3 all-gather.2.cloned.1.call-start
  548.1 99.5 %all-reduce.2.cloned.1.call-done = f32[2560,512]{1,0:T(8,128)} async-done(((f32[2560,512]{1,0:T(8,128)}), f32[2560,512]{1,0:T(8,128)}) %all-reduce.2.cloned.1.call-update) | async-done | bytes 5242896 | tf_op jit(solution)/shard_map/psum | solution.py:14
  647.6 11.9 %fusion.21 = f32[2560,512]{1,0:T(8,128)} fusion(f32[2560,512]{1,0:T(8,128)} %all-reduce.2.cloned.1.call-done, f32[512,512]{1,0:T(8,128)S(1)} %copy-done), kind=kOutput, calls=%fused_computation.90 | convolution fusion | flops 8053063680 | bytes 11534336 | tf_op jit(solution)/shard_map/dot_general | solution.py:111
  659.5 354.5 %all-gather.2.cloned.1.call-done = f32[10240,512]{1,0:T(8,128)} async-done(((f32[2560,512]{1,0:T(8,128)}), f32[10240,512]{1,0:T(8,128)}) %all-gather.2.cloned.1.call-update) | async-done | bytes 20971536 | tf_op jit(solution)/shard_map/all_gather | solution.py:117
  1014.0 26.6 %convolution_subtract_fusion = f32[2560,1280]{1,0:T(8,128)} fusion(f32[2560,1280]{1,0:T(8,128)} %bitcast_add_fusion, f32[2560,512]{1,0:T(8,128)} %fusion.21, f32[10240,512]{1,0:T(8,128)} %all-gather.2.cloned.1.call-done, s32[]{:T(128)S(6)} %select_n.210), kind=kOutput, calls=%fused_computation.9 | convolution fusion | flops 20135936000 | bytes 34078724 | tf_op jit(solution)/shard_map/dot_general | solution.py:119
  (47 shorter events, 1.6 us)
Async XLA Ops:
  7.2 640.4 %copy-start = (f32[512,512]{1,0:T(8,128)S(1)}, f32[512,512]{1,0:T(8,128)}, u32[]{:S(2)}) copy-start(f32[512,512]{1,0:T(8,128)} %param.11) | copy-start | bytes 3145732
  82.2 6.5 copy-start.1
  82.2 367.5 %all-to-all-start = ((f32[32,8,128,128]{3,2,1,0:T(8,128)}), f32[32,8,128,128]{3,2,1,0:T(8,128)}, u32[]{:S(2)}, u32[]{:S(2)}) async-start(f32[32,8,128,128]{3,2,1,0:T(8,128)} %bitcast.41), calls=%async_computation | async-start | bytes 33554432 | tf_op jit(solution)/shard_map/all_to_all | solution.py:70
  88.4 559.1 %all-reduce.2.cloned.1.call-start = ((), (), s32[]{:S(2)}) async-start(), calls=%async_computation.1 | async-start | bytes 10485760 | tf_op jit(solution)/shard_map/psum | solution.py:14
  520.7 14.2 %copy-start.2 = (f32[2560]{0:T(1024)S(1)}, f32[2560]{0:T(1024)}, u32[]{:S(2)}) copy-start(f32[2560]{0:T(1024)} %param.10) | copy-start | bytes 30724
  547.8 466.1 %all-gather.2.cloned.1.call-start = ((), (), s32[]{:S(2)}) async-start(), calls=%async_computation.2 | async-start | bytes 26214400 | tf_op jit(solution)/shard_map/all_gather | solution.py:117
Sparse Core Ops, SparseCore 0:
  547.9 99.5 all-reduce.1
  659.6 354.3 all-gather.1
where the time goes:
time: 1050 us
  waiting for transfers between devices  772 us (74%)
  local copies, waits for them, and re-layouts  146 us (14%)
  other arithmetic  69.8 us (7%)
  matrix products  38.5 us (4%)
  between operations  14.4 us (1%)
    all_gather x1, waiting for transfers between devices, on_device(): gathered = lax.all_gather(factor_panel, 'row', axis=0, tiled=True)  354 us
    all_to_all x1, waiting for transfers between devices, on_device(): lax.all_to_all(outgoing.reshape(devices_all, capacity, BLK, BLK), ('row',...  318 us
    psum x1, waiting for transfers between devices, broadcast(): return lax.psum(jnp.where(mine, shard, jnp.zeros_like(shard)), axis)  99.5 us
    scatter-add x1, other arithmetic, on_device(): assembled = jnp.zeros((dump_slot + 1, BLK, BLK), jnp.float32).at[slot_tar...  52.7 us
    scatter x1, local copies, waits for them, and re-layouts, on_device(): outgoing = jnp.zeros((slot_total, BLK, BLK), jnp.float32).at[target_dev *...  45.7 us
    scatter x1, local copies, waits for them, and re-layouts, on_device(): slot_target = jnp.full((slot_total + 1,), dump_slot, jnp.int32).at[slot_o...  30.6 us
    dot_general x1, matrix products, on_device(): lax.dot_general(factor_panel, across, (((1,), (1,)), ((), ())), precision...  26.6 us
  transfers between devices with their start and end apart: 3, of which 3 were waited for; matrix products, arithmetic and copies ran while one was open for 4% of the time, Pallas kernels for 0%

commit v1 on v0

v1 whole, which is shorter than its diff:
```python
import functools
import jax
import jax.numpy as jnp
from jax import lax
from jax.experimental import pallas as pl
from jax.experimental.pallas import tpu as pltpu
from jax.sharding import PartitionSpec as P

BLK = 128
STEP = 256
MIB = 1 << 20


def pick(flags, values):
    return jnp.sum(jnp.where(flags, values, 0), axis=-1, dtype=jnp.int32)


def split(x):
    high = x.astype(jnp.bfloat16)
    low = (x - high.astype(jnp.float32)).astype(jnp.bfloat16)
    return high, low


def dot3(ah, al, bh, bl):
    d = functools.partial(
        lax.dot_general,
        dimension_numbers=(((1,), (1,)), ((), ())),
        preferred_element_type=jnp.float32,
    )
    return d(ah, bh) + (d(ah, bl) + d(al, bh))


def ranks(owner):
    n = owner.shape[-1]
    earlier = jnp.arange(n)[:, None] > jnp.arange(n)[None, :]
    same = owner[..., :, None] == owner[..., None, :]
    return jnp.sum((same & earlier).astype(jnp.int32), axis=-1)


def selection(owner, count, each):
    rank = ranks(owner)
    wanted = (owner[None, None, :] == jnp.arange(count)[:, None, None]) & (
        rank[None, None, :] == jnp.arange(each)[None, :, None]
    )
    return pick(wanted, jnp.arange(owner.shape[0], dtype=jnp.int32))


def pack_kernel(rows_ref, cols_ref, x_ref, o_ref, *, col_count, per_col):
    for t in range(col_count):
        for w in range(per_col):
            j = cols_ref[t * per_col + w]
            o_ref[0, t, 0, w] = x_ref[:, pl.ds(pl.multiple_of(j * BLK, BLK), BLK)]


def pack(updates, rowsel, colsel, row_count, col_count, per_row, per_col):
    width = updates.shape[1]
    grid = pltpu.PrefetchScalarGridSpec(
        num_scalar_prefetch=2,
        grid=(row_count * per_row,),
        in_specs=[pl.BlockSpec((BLK, width), lambda g, r, c: (r[g], 0))],
        out_specs=pl.BlockSpec(
            (1, col_count, 1, per_col, BLK, BLK),
            lambda g, r, c: (g // per_row, 0, g % per_row, 0, 0, 0),
        ),
    )
    return pl.pallas_call(
        functools.partial(pack_kernel, col_count=col_count, per_col=per_col),
        grid_spec=grid,
        out_shape=jax.ShapeDtypeStruct(
            (row_count, col_count, per_row, per_col, BLK, BLK), jnp.float32
        ),
        compiler_params=pltpu.CompilerParams(vmem_limit_bytes=32 * MIB),
    )(rowsel.reshape(-1), colsel.reshape(-1), updates)


def block_sum(recv_ref, rtab, ctab, x, y, front_rows, front_cols):
    total = None
    for c in range(2):
        r = rtab[c * front_rows + x]
        k = ctab[c * front_cols + y]
        good = (r >= 0) & (k >= 0)
        tile = recv_ref[jnp.where(good, r + k, 0)]
        tile = jnp.where(good, tile, 0.0)
        total = tile if total is None else total + tile
    return total


def eye_mask():
    i = lax.broadcasted_iota(jnp.int32, (BLK, BLK), 0)
    j = lax.broadcasted_iota(jnp.int32, (BLK, BLK), 1)
    return i == j


def finish_kernel(rtab, ctab, dtab, recv_ref, diag_ref, factor_ref, across_ref, o_ref, ah, al,
                  *, front_rows, front_cols, chunk):
    g = pl.program_id(0)

    @pl.when(g == 0)
    def _():
        h, l = split(across_ref[...])
        ah[...] = h
        al[...] = l

    fh, fl = split(factor_ref[...])
    eye = eye_mask()
    for base in range(0, front_cols, chunk):
        rows = pl.ds(base * BLK, chunk * BLK)
        term = dot3(fh, fl, ah[rows, :], al[rows, :])
        for p in range(STEP // BLK):
            x = g * (STEP // BLK) + p
            drow = diag_ref[pl.ds(x, 1), :]
            for y in range(base, base + chunk):
                tile = block_sum(recv_ref, rtab, ctab, x, y, front_rows, front_cols)
                on = eye & (dtab[0] + x == dtab[1] + y)
                tile = tile + jnp.where(on, drow, 0.0)
                o_ref[p * BLK:(p + 1) * BLK, y * BLK:(y + 1) * BLK] = (
                    tile - term[p * BLK:(p + 1) * BLK, (y - base) * BLK:(y - base + 1) * BLK]
                )


def finish(rtab, ctab, dtab, recv, diag, factor, across):
    height, panel = factor.shape
    width = across.shape[0]
    front_rows, front_cols = height // BLK, width // BLK
    chunk = 5 if front_cols % 5 == 0 else 1
    once = dict(pipeline_mode=pl.Buffered(1))
    grid = pltpu.PrefetchScalarGridSpec(
        num_scalar_prefetch=3,
        grid=(height // STEP,),
        in_specs=[
            pl.BlockSpec(recv.shape, lambda g, *_: (0, 0, 0), **once),
            pl.BlockSpec(diag.shape, lambda g, *_: (0, 0), **once),
            pl.BlockSpec((STEP, panel), lambda g, *_: (g, 0)),
            pl.BlockSpec((width, panel), lambda g, *_: (0, 0), **once),
        ],
        out_specs=pl.BlockSpec((STEP, width), lambda g, *_: (g, 0)),
        scratch_shapes=[pltpu.VMEM((width, panel), jnp.bfloat16)] * 2,
    )
    return pl.pallas_call(
        functools.partial(finish_kernel, front_rows=front_rows, front_cols=front_cols, chunk=chunk),
        grid_spec=grid,
        out_shape=jax.ShapeDtypeStruct((height, width), jnp.float32),
        compiler_params=pltpu.CompilerParams(vmem_limit_bytes=48 * MIB),
    )(rtab, ctab, dtab, recv, diag, factor, across)


def raw_kernel(rtab, ctab, dtab, recv_ref, diag_ref, o_ref, *, front_rows, front_cols, panel_cols):
    eye = eye_mask()

    @pl.loop(0, front_rows)
    def _(x):
        drow = diag_ref[pl.ds(x, 1), :]
        for y in range(panel_cols):
            tile = block_sum(recv_ref, rtab, ctab, x, y, front_rows, front_cols)
            tile = tile + jnp.where(eye & (dtab[0] + x == dtab[1] + y), drow, 0.0)
            o_ref[pl.ds(pl.multiple_of(x * BLK, BLK), BLK), y * BLK:(y + 1) * BLK] = tile


def raw_panel_of(rtab, ctab, dtab, recv, diag, front_rows, front_cols, panel):
    smem = pl.BlockSpec(memory_space=pltpu.SMEM)
    vmem = pl.BlockSpec(memory_space=pltpu.VMEM)
    return pl.pallas_call(
        functools.partial(raw_kernel, front_rows=front_rows, front_cols=front_cols,
                          panel_cols=panel // BLK),
        in_specs=[smem, smem, smem, vmem, vmem],
        out_specs=vmem,
        out_shape=jax.ShapeDtypeStruct((front_rows * BLK, panel), jnp.float32),
        compiler_params=pltpu.CompilerParams(vmem_limit_bytes=40 * MIB),
    )(rtab, ctab, dtab, recv, diag)


def tables(block_map, row_count, col_count, row_items, col_items, front_rows, front_cols,
           per_row, per_col, my_row, my_col):
    half = col_count // 2
    child_blocks = block_map.shape[1]
    cap = per_row * per_col
    child = jnp.where(my_col >= half, block_map[1], block_map[0])
    row_parent = pick(
        (my_col % half * row_items + jnp.arange(row_items))[:, None] == jnp.arange(child_blocks)[None, :],
        child[None, :],
    )
    col_parent = pick(
        (my_row * col_items + jnp.arange(col_items))[:, None] == jnp.arange(child_blocks)[None, :],
        child[None, :],
    )
    rowsel = selection(row_parent // front_rows, row_count, per_row)
    colsel = selection(col_parent // front_cols, col_count, per_col)
    ids = jnp.arange(child_blocks, dtype=jnp.int32)
    row_rank = ranks((block_map // front_rows).reshape(2, -1, row_items)).reshape(2, -1)
    col_rank = ranks((block_map // front_cols).reshape(2, -1, col_items)).reshape(2, -1)
    source_col = jnp.arange(2, dtype=jnp.int32)[:, None] * half + ids[None, :] // row_items
    row_value = source_col * cap + row_rank * per_col
    col_value = (ids[None, :] // col_items) * (col_count * cap) + col_rank
    at_row = block_map[:, None, :] == (my_row * front_rows + jnp.arange(front_rows))[None, :, None]
    at_col = block_map[:, None, :] == (my_col * front_cols + jnp.arange(front_cols))[None, :, None]
    rtab = pick(at_row, row_value[:, None, :] + 1) - 1
    ctab = pick(at_col, col_value[:, None, :] + 1) - 1
    return rowsel, colsel, rtab.reshape(-1), ctab.reshape(-1)


def on_device(updates, block_map, own_diag, panel_inverse):
    row_count, col_count = lax.axis_size("row"), lax.axis_size("col")
    my_row, my_col = lax.axis_index("row"), lax.axis_index("col")
    devices = row_count * col_count
    row_items, col_items = updates.shape[0] // BLK, updates.shape[1] // BLK
    per_row, per_col = max(1, row_items // row_count), max(1, col_items // col_count)
    height = own_diag.shape[0]
    width = height * row_count // col_count
    panel = panel_inverse.shape[0]
    front_rows, front_cols = height // BLK, width // BLK
    rowsel, colsel, rtab, ctab = tables(
        block_map, row_count, col_count, row_items, col_items, front_rows, front_cols,
        per_row, per_col, my_row, my_col,
    )
    dtab = jnp.stack([my_row * front_rows, my_col * front_cols]).astype(jnp.int32)
    diag = own_diag.reshape(front_rows, BLK)
    outgoing = pack(updates, rowsel, colsel, row_count, col_count, per_row, per_col)
    incoming = lax.all_to_all(
        outgoing.reshape(devices, per_row * per_col, BLK, BLK),
        ("row", "col"), split_axis=0, concat_axis=0, tiled=True,
    ).reshape(-1, BLK, BLK)
    raw = raw_panel_of(rtab, ctab, dtab, incoming, diag, front_rows, front_cols, panel)
    raw = lax.psum(jnp.where(my_col == 0, raw, 0.0), "col")
    factor = lax.dot_general(
        raw, panel_inverse, (((1,), (1,)), ((), ())),
        precision=lax.Precision.HIGHEST, preferred_element_type=jnp.float32,
    )
    start = my_col * width
    mine = start // height == my_row
    across = lax.dynamic_slice_in_dim(factor, start % height, width, 0)
    across = lax.psum(jnp.where(mine, across, 0.0), "row")
    trailing = finish(rtab, ctab, dtab, incoming, diag, factor, across)
    return (factor, trailing)


def solution(mesh):
    return jax.shard_map(
        on_device,
        mesh=mesh,
        in_specs=(P("col", "row"), P(), P("row"), P()),
        out_specs=(P("row", None), P("row", "col")),
        check_vma=False,
    )
```

time: 1050 us -> 659 us (0.63)
  waiting for transfers between devices: 772 us -> 562 us
  local copies, waits for them, and re-layouts: 146 us -> 10.7 us
  other arithmetic: 69.8 us -> 7.95 us
  Pallas kernels: 0 us -> 44.1 us
  matrix products: 38.5 us -> 10.4 us
    all_gather x1 -> x0, waiting for transfers between devices: 354 us -> none  [on_device(): gathered = lax.all_gather(factor_panel, 'row', axis=0, tiled=True)]
    psum x1 -> x2, waiting for transfers between devices: 99.5 us -> 202 us  [the longest x1 103 us: on_device(): across = lax.psum(jnp.where(mine, across, 0.0), 'row')]
    scatter x2 -> x0, local copies, waits for them, and re-layouts: 76.3 us -> none  [the longest x1 45.7 us: on_device(): outgoing = jnp.zeros((slot_total, BLK, BLK), jnp.float32).at[target_dev *...]
    scatter-add x1 -> x0, other arithmetic: 52.7 us -> none  [on_device(): assembled = jnp.zeros((dump_slot + 1, BLK, BLK), jnp.float32).at[slot_tar...]
    pallas_call x0 -> x3, Pallas kernels: none -> 44.1 us  [the longest x1 23.8 us: finish(): pl.pallas_call(functools.partial(finish_kernel, front_rows=front_rows, fr...]
    all_to_all x1, waiting for transfers between devices: 318 us -> 359 us  [on_device(): lax.all_to_all(outgoing.reshape(devices, per_row * per_col, BLK, BLK), ('...]
    dot_general x2 -> x1, matrix products: 38.5 us -> 10.4 us  [on_device(): lax.dot_general(raw, panel_inverse, (((1,), (1,)), ((), ())), precision=l...]
    broadcast_in_dim x2 -> x0, local copies, waits for them, and re-layouts: 14.2 us -> none  [the longest x1 7.84 us: on_device(): jnp.zeros((slot_total, BLK, BLK), jnp.float32)]
  transfers between devices with their start and end apart: 3 -> 3, of which waited for: 3 -> 3; matrix products, arithmetic and copies ran while one was open for 4% -> 0% of each run, Pallas kernels for 0% -> 0%
where the time goes in v1:
time: 659 us; the launch traced here: 655 us
  waiting for transfers between devices  562 us (85%)
  Pallas kernels  44.1 us (7%)
  between operations  14.3 us (2%)
  local copies, waits for them, and re-layouts  10.7 us (2%)
  matrix products  10.4 us (2%)
  other arithmetic  7.95 us (1%)
    all_to_all x1, waiting for transfers between devices, on_device(): lax.all_to_all(outgoing.reshape(devices, per_row * per_col, BLK, BLK), ('...  359 us
    psum x1, waiting for transfers between devices, on_device(): across = lax.psum(jnp.where(mine, across, 0.0), 'row')  103 us
    psum x1, waiting for transfers between devices, on_device(): raw = lax.psum(jnp.where(my_col == 0, raw, 0.0), 'col')  99.7 us
    pallas_call x1, Pallas kernels, finish(): pl.pallas_call(functools.partial(finish_kernel, front_rows=front_rows, fr...  23.8 us
    pallas_call x1, Pallas kernels, pack(): pl.pallas_call(functools.partial(pack_kernel, col_count=col_count, per_co...  13.2 us
  transfers between devices with their start and end apart: 3, of which 3 were waited for; matrix products, arithmetic and copies ran while one was open for 0% of the time, Pallas kernels for 0%

profile of v1, /device:TPU:8, one launch (start us, length us, event | category | flops | bytes accessed | tf_op | source)
XLA Modules:
  0.0 655.1 jit_solution(16992625680031761454)
XLA Ops:
  7.2 0.8 fusion.2
  8.0 0.2 select_reduce_fusion.1
  8.2 0.2 convert_reduce_fusion.2
  8.4 0.2 convert_reduce_fusion.3
  8.6 0.2 select_reduce_fusion.2
  8.8 0.1 reshape.316.rows_ref
  8.8 0.1 select_reduce_fusion
  9.0 0.1 copy.11
  9.1 0.1 reshape.317.cols_ref
  9.2 13.2 %shard_map.59 = f32[4,8,4,2,128,128]{5,4,3,2,1,0:T(8,128)S(1)} custom-call(s32[16]{0:T(128)S(1)} %reshape.316.rows_ref, s32[16]{0:T(128)S(1)} %reshape.317.cols_ref, f32[2048,2048]{1,0:T(8,128)} %x_ref.1), custom_call_target="tpu_custom_call" | custom-call | tf_op jit(solution)/shard_map/pallas_call | solution.py:66
  22.4 5.7 copy-done.1
  28.1 6.0 all-to-all-start
  34.3 0.1 eq.193
  34.4 0.4 convert_reduce_fusion
  34.9 0.1 reshape.315
  35.0 0.1 mul.65
  35.1 0.3 fusion.1
  35.4 0.1 copy.13
  35.5 0.1 sub.48.ctab
  35.7 0.5 fusion
  36.2 0.1 copy.12
  36.2 0.1 sub.45.rtab
  36.4 359.1 %all-to-all-done = f32[32,8,128,128]{3,2,1,0:T(8,128)} async-done(((f32[32,8,128,128]{3,2,1,0:T(8,128)}), f32[32,8,128,128]{3,2,1,0:T(8,128)}, u32[]{:S(2)}, u32[]{:S(2)}) %all-to-all-start) | async-done | bytes 16777248 | tf_op jit(solution)/shard_map/all_to_all | solution.py:218
  395.5 7.0 %shard_map.60 = f32[2560,512]{1,0:T(8,128)S(1)} custom-call(s32[40]{0:T(128)S(1)} %sub.45.rtab, s32[20]{0:T(128)S(1)} %sub.48.ctab, s32[2]{0:T(128)S(1)} %pad_add_fusion.dtab, f32[256,128,128]{2,1,0:T(8,128)} %bitcast.4.recv_ref, f32[20,128]{1,0:T(8,128)S(1)} %bitcast.10), custom_call_target="tpu_custom_call" | custom-call | tf_op jit(solution)/shard_map/pallas_call | solution.py:162
  402.5 3.0 broadcast_select_fusion
  405.6 99.7 %all-reduce.3.cloned.1.call-done = f32[2560,512]{1,0:T(8,128)} async-done(((f32[2560,512]{1,0:T(8,128)}), f32[2560,512]{1,0:T(8,128)}) %all-reduce.3.cloned.1.call-update) | async-done | bytes 5242896 | tf_op jit(solution)/shard_map/psum | solution.py:223
  505.3 10.4 %fusion.3.factor_ref = f32[2560,512]{1,0:T(8,128)S(1)} fusion(f32[2560,512]{1,0:T(8,128)} %all-reduce.3.cloned.1.call-done, f32[512,512]{1,0:T(8,128)S(1)} %copy-done), kind=kOutput, calls=%fused_computation.44 | convolution fusion | flops 8053063680 | bytes 11534336 | tf_op jit(solution)/shard_map/dot_general | solution.py:224
  515.7 2.3 copy-done.4
  518.1 1.8 dynamic-slice_select_fusion
  520.0 102.8 %all-reduce.5.cloned.1.call-done.across_ref = f32[1280,512]{1,0:T(8,128)} async-done(((f32[1280,512]{1,0:T(8,128)}), f32[1280,512]{1,0:T(8,128)}) %all-reduce.5.cloned.1.call-update) | async-done | bytes 2621456 | tf_op jit(solution)/shard_map/psum | solution.py:231
  622.7 1.7 copy-done.2
  624.5 23.8 %shard_map.61 = f32[2560,1280]{1,0:T(8,128)} custom-call(s32[40]{0:T(128)S(1)} %sub.45.rtab, s32[20]{0:T(128)S(1)} %sub.48.ctab, s32[2]{0:T(128)S(1)} %pad_add_fusion.dtab, f32[256,128,128]{2,1,0:T(8,128)} %bitcast.4.recv_ref, f32[20,128]{1,0:T(8,128)S(1)} %bitcast.11, f32[2560,512]{1,0:T(8,128)} %copy-done.4, f32[1280,512]{1,0:T(8,128)S(1)} %copy-done.2), custom_call_target="tpu_custom_call" | custom-call | tf_op jit(solution)/shard_map/pallas_call | solution.py:139
  (34 shorter events, 0.5 us)
Async XLA Ops:
  7.2 498.2 %copy-start = (f32[512,512]{1,0:T(8,128)S(1)}, f32[512,512]{1,0:T(8,128)}, u32[]{:S(2)}) copy-start(f32[512,512]{1,0:T(8,128)} %param.7) | copy-start | bytes 3145732
  22.4 5.7 copy-start.1
  28.1 6.1 copy-start.5
  28.1 367.4 %copy-start.3 = (f32[2560]{0:T(1024)S(1)}, f32[2560]{0:T(1024)}, u32[]{:S(2)}) copy-start(f32[2560]{0:T(1024)} %param.6) | copy-start | bytes 30724
  28.1 367.4 %all-to-all-start = ((f32[32,8,128,128]{3,2,1,0:T(8,128)}), f32[32,8,128,128]{3,2,1,0:T(8,128)}, u32[]{:S(2)}, u32[]{:S(2)}) async-start(f32[32,8,128,128]{3,2,1,0:T(8,128)} %bitcast.9), calls=%async_computation | async-start | bytes 33554432 | tf_op jit(solution)/shard_map/all_to_all | solution.py:218
  34.2 471.2 %all-reduce.3.cloned.1.call-start = ((), (), s32[]{:S(2)}) async-start(), calls=%async_computation.1 | async-start | bytes 10485760 | tf_op jit(solution)/shard_map/psum | solution.py:223
  405.5 217.2 %all-reduce.5.cloned.1.call-start = ((), (), s32[]{:S(2)}) async-start(), calls=%async_computation.2 | async-start | bytes 5242880 | tf_op jit(solution)/shard_map/psum | solution.py:231
  515.7 2.4 copy-start.4
  622.7 1.7 copy-start.2
Sparse Core Ops, SparseCore 0:
  405.6 99.6 all-reduce.2
  520.1 102.6 all-reduce.4

commit v2 on v1

--- a/solution.py
+++ b/solution.py
@@ -91,7 +91,7 @@
     return i == j
 
 
-def finish_kernel(rtab, ctab, dtab, recv_ref, diag_ref, factor_ref, across_ref, o_ref, ah, al,
+def finish_kernel(rtab, ctab, dtab, recv_ref, diag_ref, factor_ref, across_ref, copy_ref, o_ref, ah, al,
                   *, front_rows, front_cols, chunk):
     g = pl.program_id(0)
 
@@ -101,7 +101,9 @@
         ah[...] = h
         al[...] = l
 
-    fh, fl = split(factor_ref[...])
+    f = factor_ref[...]
+    copy_ref[...] = f
+    fh, fl = split(f)
     eye = eye_mask()
     for base in range(0, front_cols, chunk):
         rows = pl.ds(base * BLK, chunk * BLK)
@@ -133,40 +135,271 @@
             pl.BlockSpec((STEP, panel), lambda g, *_: (g, 0)),
             pl.BlockSpec((width, panel), lambda g, *_: (0, 0), **once),
         ],
-        out_specs=pl.BlockSpec((STEP, width), lambda g, *_: (g, 0)),
+        out_specs=[
+            pl.BlockSpec((STEP, panel), lambda g, *_: (g, 0)),
+            pl.BlockSpec((STEP, width), lambda g, *_: (g, 0)),
+        ],
         scratch_shapes=[pltpu.VMEM((width, panel), jnp.bfloat16)] * 2,
     )
     return pl.pallas_call(
         functools.partial(finish_kernel, front_rows=front_rows, front_cols=front_cols, chunk=chunk),
         grid_spec=grid,
-        out_shape=jax.ShapeDtypeStruct((height, width), jnp.float32),
+        out_shape=[
+            jax.ShapeDtypeStruct((height, panel), jnp.float32),
+            jax.ShapeDtypeStruct((height, width), jnp.float32),
+        ],
         compiler_params=pltpu.CompilerParams(vmem_limit_bytes=48 * MIB),
     )(rtab, ctab, dtab, recv, diag, factor, across)
 
 
-def raw_kernel(rtab, ctab, dtab, recv_ref, diag_ref, o_ref, *, front_rows, front_cols, panel_cols):
-    eye = eye_mask()
-
-    @pl.loop(0, front_rows)
-    def _(x):
-        drow = diag_ref[pl.ds(x, 1), :]
-        for y in range(panel_cols):
-            tile = block_sum(recv_ref, rtab, ctab, x, y, front_rows, front_cols)
-            tile = tile + jnp.where(eye & (dtab[0] + x == dtab[1] + y), drow, 0.0)
-            o_ref[pl.ds(pl.multiple_of(x * BLK, BLK), BLK), y * BLK:(y + 1) * BLK] = tile
-
-
-def raw_panel_of(rtab, ctab, dtab, recv, diag, front_rows, front_cols, panel):
+def exchange_kernel(rtab, ctab, send_ref, diag_ref, inv_ref, recv_ref, factor_ref, across_ref,
+                    stage, raw, fact, chunks, inv_high, inv_low,
+                    out_sem, in_sem, self_sem, stage_sem, scatter_send, scatter_recv,
+                    z_send, z_recv, row_send, row_recv, a_send, a_recv, local_sem, a_local,
+                    *, rows_n, cols_n, front_rows, front_cols, panel_cols):
+    r, c = lax.axis_index("row"), lax.axis_index("col")
+    total = rows_n * cols_n
+    me = r * cols_n + c
+    half = cols_n // 2
+    ratio = cols_n // rows_n
+    per_width = cols_n // ratio
+    size = chunks.shape[1]
+    mesh_id = pl.DeviceIdType.MESH
+
+    def each(count, body):
+        def step(n, carry):
+            body(n)
+            return carry
+        lax.fori_loop(0, count, step, 0)
+
+    def at(k):
+        return pl.ds(pl.multiple_of(k * size, 8), size)
+
+    barrier = pltpu.get_barrier_semaphore()
+
+    def greet(n):
+        t = lax.rem(me + n + 1, total)
+        pl.semaphore_signal(barrier, inc=1, device_id=(t // cols_n, lax.rem(t, cols_n)),
+                            device_id_type=mesh_id)
+    each(total - 1, greet)
+    pl.semaphore_wait(barrier, total - 1)
+
+    def tiles(t_row, t_col, source, t):
+        return pltpu.make_async_remote_copy(
+            src_ref=send_ref.at[t], dst_ref=recv_ref.at[source],
+            send_sem=out_sem.at[t], recv_sem=in_sem.at[source],
+            device_id=(t_row, t_col), device_id_type=mesh_id)
+
+    def send(n):
+        g, i = n // half, lax.rem(n, half)
+        t_col = 2 * lax.rem(i + c // 2, half) + g // rows_n
+        t_row = lax.rem(r + g + i, rows_n)
+        t = t_row * cols_n + t_col
+
+        @pl.when(t != me)
+        def _():
+            tiles(t_row, t_col, me, t).start()
+    each(total, send)
+    own = pltpu.make_async_copy(send_ref.at[me], recv_ref.at[me], self_sem)
+    own.start()
+
+    def wait_tiles():
+        def one(n):
+            t = lax.rem(me + n + 1, total)
+            tiles(t // cols_n, lax.rem(t, cols_n), t, t).wait_recv()
+        each(total - 1, one)
+        own.wait()
+
+    def scatter(k):
+        return pltpu.make_async_remote_copy(
+            src_ref=fact.at[at(k), :], dst_ref=chunks.at[r],
+            send_sem=scatter_send.at[k], recv_sem=scatter_recv,
+            device_id=(r, k), device_id_type=mesh_id)
+
+    whole = pltpu.make_async_copy(fact, factor_ref, local_sem)
+
+    @pl.when(c == 0)
+    def _():
+        wait_tiles()
+        load = pltpu.make_async_copy(recv_ref, stage, stage_sem)
+        load.start()
+        h, l = split(inv_ref[...])
+        inv_high[...] = h
+        inv_low[...] = l
+        load.wait()
+        eye = eye_mask()
+        cap = stage.shape[1]
+
+        def assemble(x):
+            drow = diag_ref[pl.ds(x, 1), :]
+            for y in range(panel_cols):
+                tile = jnp.where(eye & (r * front_rows + x == y), drow, 0.0)
+                for child in range(2):
+                    a = rtab[child * front_rows + x]
+                    b = ctab[child * front_cols + y]
+                    good = (a >= 0) & (b >= 0)
+                    slot = jnp.where(good, a + b, 0)
+                    tile = tile + jnp.where(good, stage[slot // cap, lax.rem(slot, cap)], 0.0)
+                raw[pl.ds(pl.multiple_of(x * BLK, BLK), BLK), y * BLK:(y + 1) * BLK] = tile
+        each(front_rows, assemble)
+
+        def multiply(n):
+            k = cols_n - 1 - n
+            h, l = split(raw[at(k), :])
+            fact[at(k), :] = dot3(h, l, inv_high[...], inv_low[...])
+
+            @pl.when(k != 0)
+            def _():
+                scatter(k).start()
+        each(cols_n, multiply)
+        chunks[r] = fact[0:size, :]
+        whole.start()
+
+    @pl.when(c != 0)
+    def _():
+        scatter(c).wait_recv()
+
+    def along_z(peer, slot):
+        return pltpu.make_async_remote_copy(
+            src_ref=chunks.at[r], dst_ref=chunks.at[slot],
+            send_sem=z_send.at[peer], recv_sem=z_recv.at[slot],
+            device_id=(peer, c), device_id_type=mesh_id)
+
+    def z_start(n):
+        along_z(lax.rem(r + n + 1, rows_n), r).start()
+    each(rows_n - 1, z_start)
+
+    def along_row(peer, source):
+        return pltpu.make_async_remote_copy(
+            src_ref=chunks.at[r], dst_ref=factor_ref.at[at(source), :],
+            send_sem=row_send.at[peer], recv_sem=row_recv.at[source],
+            device_id=(r, peer), device_id_type=mesh_id)
+
+    def row_start(n):
+        peer = lax.rem(c + n + 1, cols_n)
+
+        @pl.when(peer != 0)
+        def _():
+            along_row(peer, c).start()
+    each(cols_n - 1, row_start)
+    mine = pltpu.make_async_copy(chunks.at[r], factor_ref.at[at(c), :], local_sem)
+
+    @pl.when(c != 0)
+    def _():
+        mine.start()
+
+    def match(k, slot):
+        return pltpu.make_async_remote_copy(
+            src_ref=chunks.at[k], dst_ref=across_ref.at[at(slot), :],
+            send_sem=a_send.at[k], recv_sem=a_recv.at[slot],
+            device_id=(r, ratio * k + c // per_width), device_id_type=mesh_id)
+
+    def match_own(k):
+        return pltpu.make_async_copy(
+            chunks.at[k], across_ref.at[at(lax.rem(c, per_width)), :], a_local)
+
+    def forward(n):
+        k = lax.rem(r + n, rows_n)
+
+        @pl.when(n != 0)
+        def _():
+            along_z(k, k).wait_recv()
+        t = ratio * k + c // per_width
+
+        @pl.when(t != c)
+        def _():
+            match(k, lax.rem(c, per_width)).start()
+
+        @pl.when(t == c)
+        def _():
+            match_own(k).start()
+    each(rows_n, forward)
+
+    @pl.when(c != 0)
+    def _():
+        def from_row(n):
+            peer = lax.rem(c + n + 1, cols_n)
+            along_row(peer, peer).wait_recv()
+        each(cols_n - 1, from_row)
+        mine.wait()
+        wait_tiles()
+
+    @pl.when(c == 0)
+    def _():
+        whole.wait()
+        each(cols_n - 1, lambda n: scatter(n + 1).wait_send())
+
+    def from_match(i):
+        source = lax.rem(c, ratio) * per_width + i
+
+        @pl.when(source != c)
+        def _():
+            match(c // ratio, i).wait_recv()
+
+        @pl.when(source == c)
+        def _():
+            match_own(c // ratio).wait()
+    each(per_width, from_match)
+
+    def sent_row(n):
+        peer = lax.rem(c + n + 1, cols_n)
+
+        @pl.when(peer != 0)
+        def _():
+            along_row(peer, c).wait_send()
+    each(cols_n - 1, sent_row)
+
+    def sent_z(n):
+        along_z(lax.rem(r + n + 1, rows_n), r).wait_send()
+    each(rows_n - 1, sent_z)
+
+    def sent_match(k):
+        @pl.when(ratio * k + c // per_width != c)
+        def _():
+            match(k, lax.rem(c, per_width)).wait_send()
+    each(rows_n, sent_match)
+
+    def sent_tiles(n):
+        t = lax.rem(me + n + 1, total)
+        tiles(t // cols_n, lax.rem(t, cols_n), me, t).wait_send()
+    each(total - 1, sent_tiles)
+
+
+def exchange(rtab, ctab, outgoing, diag, inverse, rows_n, cols_n, width):
+    front_rows = diag.shape[0]
+    height, panel = front_rows * BLK, inverse.shape[0]
+    ratio = cols_n // rows_n
     smem = pl.BlockSpec(memory_space=pltpu.SMEM)
     vmem = pl.BlockSpec(memory_space=pltpu.VMEM)
+    hbm = pl.BlockSpec(memory_space=pl.ANY)
+    dma = pltpu.SemaphoreType.DMA
     return pl.pallas_call(
-        functools.partial(raw_kernel, front_rows=front_rows, front_cols=front_cols,
-                          panel_cols=panel // BLK),
-        in_specs=[smem, smem, smem, vmem, vmem],
-        out_specs=vmem,
-        out_shape=jax.ShapeDtypeStruct((front_rows * BLK, panel), jnp.float32),
-        compiler_params=pltpu.CompilerParams(vmem_limit_bytes=40 * MIB),
-    )(rtab, ctab, dtab, recv, diag)
+        functools.partial(exchange_kernel, rows_n=rows_n, cols_n=cols_n, front_rows=front_rows,
+                          front_cols=width // BLK, panel_cols=panel // BLK),
+        in_specs=[smem, smem, hbm, vmem, vmem],
+        out_specs=[hbm, hbm, hbm],
+        out_shape=[
+            jax.ShapeDtypeStruct(outgoing.shape, jnp.float32),
+            jax.ShapeDtypeStruct((height, panel), jnp.float32),
+            jax.ShapeDtypeStruct((width, panel), jnp.float32),
+        ],
+        scratch_shapes=[
+            pltpu.VMEM(outgoing.shape, jnp.float32),
+            pltpu.VMEM((height, panel), jnp.float32),
+            pltpu.VMEM((height, panel), jnp.float32),
+            pltpu.VMEM((rows_n, height // cols_n, panel), jnp.float32),
+            pltpu.VMEM((panel, panel), jnp.bfloat16),
+            pltpu.VMEM((panel, panel), jnp.bfloat16),
+            dma((rows_n * cols_n,)), dma((rows_n * cols_n,)), dma, dma,
+            dma((cols_n,)), dma,
+            dma((rows_n,)), dma((rows_n,)),
+            dma((cols_n,)), dma((cols_n,)),
+            dma((rows_n,)), dma((cols_n // ratio,)),
+            dma, dma,
+        ],
+        compiler_params=pltpu.CompilerParams(
+            collective_id=0, has_side_effects=True, vmem_limit_bytes=56 * MIB),
+    )(rtab, ctab, outgoing, diag, inverse)
 
 
 def tables(block_map, row_count, col_count, row_items, col_items, front_rows, front_cols,
@@ -215,22 +448,12 @@
     dtab = jnp.stack([my_row * front_rows, my_col * front_cols]).astype(jnp.int32)
     diag = own_diag.reshape(front_rows, BLK)
     outgoing = pack(updates, rowsel, colsel, row_count, col_count, per_row, per_col)
-    incoming = lax.all_to_all(
-        outgoing.reshape(devices, per_row * per_col, BLK, BLK),
-        ("row", "col"), split_axis=0, concat_axis=0, tiled=True,
-    ).reshape(-1, BLK, BLK)
-    raw = raw_panel_of(rtab, ctab, dtab, incoming, diag, front_rows, front_cols, panel)
-    raw = lax.psum(jnp.where(my_col == 0, raw, 0.0), "col")
-    factor = lax.dot_general(
-        raw, panel_inverse, (((1,), (1,)), ((), ())),
-        precision=lax.Precision.HIGHEST, preferred_element_type=jnp.float32,
-    )
-    start = my_col * width
-    mine = start // height == my_row
-    across = lax.dynamic_slice_in_dim(factor, start % height, width, 0)
-    across = lax.psum(jnp.where(mine, across, 0.0), "row")
-    trailing = finish(rtab, ctab, dtab, incoming, diag, factor, across)
-    return (factor, trailing)
+    incoming, factor, across = exchange(
+        rtab, ctab, outgoing.reshape(devices, per_row * per_col, BLK, BLK), diag, panel_inverse,
+        row_count, col_count, width,
+    )
+    incoming = incoming.reshape(-1, BLK, BLK)
+    return tuple(finish(rtab, ctab, dtab, incoming, diag, factor, across))
 
 
 def solution(mesh):

time: 659 us -> 535 us (0.81)
  waiting for transfers between devices: 562 us -> 0 us
  Pallas kernels: 44.1 us -> 519 us
  between operations: 14.3 us -> 0.79 us
  matrix products: 10.4 us -> 0 us
    pallas_call x1, Pallas kernels: 7.02 us -> 482 us  [exchange(): pl.pallas_call(functools.partial(exchange_kernel, rows_n=rows_n, cols_n=c...]
    all_to_all x1 -> x0, waiting for transfers between devices: 359 us -> none  [on_device(): lax.all_to_all(outgoing.reshape(devices, per_row * per_col, BLK, BLK), ('...]
    psum x2 -> x0, waiting for transfers between devices: 202 us -> none  [the longest x1 103 us: on_device(): across = lax.psum(jnp.where(mine, across, 0.0), 'row')]
    dot_general x1 -> x0, matrix products: 10.4 us -> none  [on_device(): lax.dot_general(raw, panel_inverse, (((1,), (1,)), ((), ())), precision=l...]
  transfers between devices with their start and end apart: 3 -> 0, of which waited for: 3 -> 0; matrix products, arithmetic and copies ran while one was open for 0% -> 0% of each run, Pallas kernels for 0% -> 0%
where the time goes in v2:
time: 535 us
  Pallas kernels  519 us (97%)
  local copies, waits for them, and re-layouts  9.4 us (2%)
    pallas_call x1, Pallas kernels, exchange(): pl.pallas_call(functools.partial(exchange_kernel, rows_n=rows_n, cols_n=c...  482 us
    pallas_call x1, Pallas kernels, finish(): pl.pallas_call(functools.partial(finish_kernel, front_rows=front_rows, fr...  23.7 us
    pallas_call x1, Pallas kernels, pack(): pl.pallas_call(functools.partial(pack_kernel, col_count=col_count, per_co...  13.2 us

profile of v2, /device:TPU:8, one launch (start us, length us, event | category | flops | bytes accessed | tf_op | source)
XLA Modules:
  0.0 534.5 jit_solution(2171568093559841086)
XLA Ops:
  0.7 0.8 fusion.2
  1.4 0.2 select_reduce_fusion.1
  1.6 0.2 convert_reduce_fusion.2
  1.8 0.1 select_reduce_fusion
  2.0 0.2 convert_reduce_fusion.3
  2.2 0.1 pad_add_fusion.dtab
  2.3 0.2 select_reduce_fusion.2
  2.4 0.1 reshape.316.rows_ref
  2.5 0.7 and_select_fusion.3
  3.2 0.1 eq.185
  3.3 0.1 copy.11
  3.4 0.1 reshape.317.cols_ref
  3.5 0.1 eq.192
  3.6 0.5 convert_reduce_fusion
  4.0 0.1 reshape.315
  4.1 0.1 mul.62
  4.2 0.1 add_add_fusion.1
  4.3 1.0 fusion.1
  5.3 0.1 copy.13
  5.4 0.6 sub.44.ctab
  6.0 1.2 fusion
  7.1 0.1 copy.12
  7.2 0.6 sub.41.rtab
  7.8 13.2 %shard_map.59 = f32[4,8,4,2,128,128]{5,4,3,2,1,0:T(8,128)S(1)} custom-call(s32[16]{0:T(128)S(1)} %reshape.316.rows_ref, s32[16]{0:T(128)S(1)} %reshape.317.cols_ref, f32[2048,2048]{1,0:T(8,128)} %x_ref.1), custom_call_target="tpu_custom_call" | custom-call | tf_op jit(solution)/shard_map/pallas_call | solution.py:66
  21.1 0.0 copy-start
  21.1 5.7 %copy-done = f32[4,8,4,2,128,128]{5,4,3,2,1,0:T(8,128)} copy-done((f32[4,8,4,2,128,128]{5,4,3,2,1,0:T(8,128)}, f32[4,8,4,2,128,128]{5,4,3,2,1,0:T(8,128)S(1)}, u32[]{:S(2)}) %copy-start) | copy-done | bytes 16777240
  26.8 482.2 %shard_map.60 = (f32[32,8,128,128]{3,2,1,0:T(8,128)}, f32[2560,512]{1,0:T(8,128)}, f32[1280,512]{1,0:T(8,128)}) custom-call(s32[40]{0:T(128)} %sub.41.rtab, s32[20]{0:T(128)} %sub.44.ctab, f32[32,8,128,128]{3,2,1,0:T(8,128)} %bitcast.7, f32[20,128]{1,0:T(8,128)} %bitcast.8, f32[512,512]{1,0:T(8,128)} %inv_ref.1), custom_call_target="tpu_custom_call" | custom-call | tf_op jit(solution)/shard_map/pallas_call | solution.py:376
  509.0 0.0 copy-done.2
  509.0 0.0 copy-done.3
  509.0 0.0 copy-done.4
  509.1 1.7 copy-done.1
  510.8 23.7 %shard_map.61 = (f32[2560,512]{1,0:T(8,128)}, f32[2560,1280]{1,0:T(8,128)}) custom-call(s32[40]{0:T(128)S(1)} %copy-done.4, s32[20]{0:T(128)S(1)} %copy-done.3, s32[2]{0:T(128)S(1)} %pad_add_fusion.dtab, f32[256,128,128]{2,1,0:T(8,128)} %bitcast.10, f32[20,128]{1,0:T(8,128)S(1)} %bitcast.9, f32[2560,512]{1,0:T(8,128)} %get-tuple-element.6.factor_ref, ...), custom_call_target="tpu_custom_call" | custom-call | tf_op jit(solution)/shard_map/pallas_call | solution.py:144
  (21 shorter events, 0.1 us)
Async XLA Ops:
  21.1 5.7 %copy-start = (f32[4,8,4,2,128,128]{5,4,3,2,1,0:T(8,128)}, f32[4,8,4,2,128,128]{5,4,3,2,1,0:T(8,128)S(1)}, u32[]{:S(2)}) copy-start(f32[4,8,4,2,128,128]{5,4,3,2,1,0:T(8,128)S(1)} %shard_map.59) | copy-start | bytes 50331652
  26.8 482.3 %copy-start.2 = (f32[2560]{0:T(1024)S(1)}, f32[2560]{0:T(1024)}, u32[]{:S(2)}) copy-start(f32[2560]{0:T(1024)} %param.6) | copy-start | bytes 30724
  26.8 482.3 %copy-start.3 = (s32[20]{0:T(128)S(1)}, s32[20]{0:T(128)}, u32[]{:S(2)}) copy-start(s32[20]{0:T(128)} %sub.44.ctab) | copy-start | bytes 244
  26.8 482.3 %copy-start.4 = (s32[40]{0:T(128)S(1)}, s32[40]{0:T(128)}, u32[]{:S(2)}) copy-start(s32[40]{0:T(128)} %sub.41.rtab) | copy-start | bytes 484
  509.0 1.7 copy-start.1
